TPU v7x, 32 devices: a whole 2x2x4 slice. The times are simulated.
32 devices in a mesh: energy: 2 (over x), slab: 8 (over z, y), row: 2 (over core).
Axes of the slice: x: 2, y: 2, z: 4, core: 2. Of those that a mesh axis runs over, the one named last changes fastest.
Arguments:
- green_blocks: bfloat16 [2, 12288, 768], P(None, ('energy', 'slab', 'row')), parts along dimension 1, may hold values from -3 to 3
- coupling: bfloat16 [2, 1024, 128], P(None, 'slab'), may hold values from -2 to 2
- source: bfloat16 [2, 12288, 128], P(None, ('energy', 'slab', 'row')), parts along dimension 1, may hold values from -6 to 6
- interior_count: int32 [8], P('slab'), may hold values from 256 to 512, as said below
Outputs:
- solution: float32 [2, 12288, 128], P(None, ('energy', 'slab', 'row')), parts along dimension 1
There are 2 independent parts, one for each index of `energy`. A program takes and returns all parts, laid end to end along the dimension named above; an argument that names none is the same for every part. Nothing has to cross between parts.
Inputs may be any that keep to these rules, and one draw needn't show every extreme that they name: `interior_count`: some slab has exactly 512 live interior orbitals.
All inputs are finite; a program needn't handle non-finite values.
Results may differ from a plain program's by a relative error of at most 0.0095.
Values may be sent and summed in bfloat16 or wider, within the bound.
A program may use at most 128 MiB of HBM per device.

v0:
```python
import jax
import jax.numpy as jnp
from jax import lax
from jax.sharding import PartitionSpec as P


def passed_along(block, axis, distance):
    devices = range(lax.axis_size(axis))
    route = [(i - distance, i) for i in devices if i - distance in devices]
    return lax.ppermute(block, axis, route)


def carried_in(part, axis, combine, identity, reverse):
    count = lax.axis_size(axis)
    place = lax.axis_index(axis)
    ahead = count - 1 - place if reverse else place
    gathered = jax.tree.map(lambda a: lax.all_gather(a, axis), part)
    state = jax.tree.map(lambda a, e: jnp.zeros_like(a) + jnp.asarray(e, a.dtype), part, identity)

    def one(step, state):
        source = count - 1 - step if reverse else step
        return combine(
            state, jax.tree.map(lambda a: lax.dynamic_index_in_dim(a, source, 0, False), gathered)
        )

    return lax.fori_loop(0, ahead, one, state)


def multiply(matrix, operand):
    return jnp.dot(
        matrix, operand, preferred_element_type=jnp.float32, precision=lax.Precision.HIGHEST
    )


def complex_product(matrix, operand):
    real_part = multiply(matrix[0], operand[0]) - multiply(matrix[1], operand[1])
    imag_part = multiply(matrix[0], operand[1]) + multiply(matrix[1], operand[0])
    return jnp.stack([real_part, imag_part])


def adjoint(matrix):
    return jnp.stack([matrix[0].T, -matrix[1].T])


def compose(earlier, later):
    return (complex_product(later[0], earlier[0]), complex_product(later[0], earlier[1]) + later[1])


def body(green_blocks, coupling, source, interior_count):
    shard_rows = green_blocks.shape[1]
    block_width = green_blocks.shape[2]
    surface_width = coupling.shape[1]
    column_count = source.shape[2]
    row_index = lax.axis_index("row")
    slab_index = lax.axis_index("slab")
    slab_count = lax.axis_size("slab")
    orbital = row_index * shard_rows + lax.iota(jnp.int32, shard_rows)
    live = (
        (orbital < surface_width + interior_count[0]) | (orbital >= block_width - surface_width)
    ).astype(jnp.float32)
    masked = (source.astype(jnp.float32) * live[None, :, None]).astype(jnp.bfloat16)
    direct = complex_product(green_blocks, lax.all_gather(masked, "row", axis=1, tiled=True))
    offset = row_index * (shard_rows - surface_width)
    own_green = lax.dynamic_slice_in_dim(green_blocks, offset, surface_width, 1)
    own_corner = jnp.concatenate(
        [own_green[:, :, :surface_width], own_green[:, :, block_width - surface_width :]], axis=2
    ).astype(jnp.float32)
    own_direct = lax.dynamic_slice_in_dim(direct, offset, surface_width, 1)
    corners, edges = (
        lax.all_gather(own_corner.astype(jnp.bfloat16), "row", axis=1, tiled=True).astype(
            own_corner.dtype
        ),
        lax.all_gather(own_direct.astype(jnp.bfloat16), "row", axis=1, tiled=True).astype(
            own_direct.dtype
        ),
    )
    green_ff = corners[:, :surface_width, :surface_width]
    green_fl = corners[:, :surface_width, surface_width:]
    green_lf = corners[:, surface_width:, :surface_width]
    green_ll = corners[:, surface_width:, surface_width:]
    edge_first = edges[:, :surface_width]
    edge_last = edges[:, surface_width:]
    right_live = (slab_index < slab_count - 1).astype(jnp.float32)
    couple_next = coupling.astype(jnp.float32) * right_live
    first_next = passed_along(edge_first.astype(jnp.bfloat16), "slab", -1).astype(edge_first.dtype)
    couple_prev = passed_along(coupling, "slab", 1).astype(jnp.float32)
    adjoint_prev = adjoint(couple_prev)
    forward_map = complex_product(green_lf, adjoint_prev)
    forward_term = edge_last + complex_product(green_ll, complex_product(couple_next, first_next))
    unit_matrix = jnp.stack(
        [
            jnp.eye(surface_width, dtype=jnp.float32),
            jnp.zeros((surface_width, surface_width), jnp.float32),
        ]
    )
    half_count = column_count // 2
    forward_part = lax.dynamic_slice_in_dim(forward_term, row_index * half_count, half_count, 2)
    start_vector = jnp.zeros(forward_part.shape, jnp.float32)
    before_part = carried_in(
        (forward_map, forward_part), "slab", compose, (unit_matrix, start_vector), False
    )[1]
    preceding_slab = lax.all_gather(
        before_part.astype(jnp.bfloat16), "row", axis=2, tiled=True
    ).astype(before_part.dtype)
    lower = complex_product(adjoint_prev, preceding_slab)
    reverse_mapping = complex_product(green_fl, couple_next)
    backward_term = edge_first + complex_product(green_ff, lower)
    backward_part = lax.dynamic_slice_in_dim(backward_term, row_index * half_count, half_count, 2)
    after_part = carried_in(
        (reverse_mapping, backward_part), "slab", compose, (unit_matrix, start_vector), True
    )[1]
    after = lax.all_gather(after_part.astype(jnp.bfloat16), "row", axis=2, tiled=True).astype(
        after_part.dtype
    )
    upper = complex_product(couple_next, after)
    lower_round = lower.astype(jnp.bfloat16)
    upper_round = upper.astype(jnp.bfloat16)
    result = direct + complex_product(green_blocks[:, :, :surface_width], lower_round)
    result = result + complex_product(
        green_blocks[:, :, block_width - surface_width :], upper_round
    )
    return result * live[None, :, None]


def solution(mesh):
    placed = (
        P(None, ("energy", "slab", "row"), None),
        P(None, "slab", None),
        P(None, ("energy", "slab", "row"), None),
        P("slab"),
    )
    return jax.shard_map(
        body,
        mesh=mesh,
        in_specs=placed,
        out_specs=P(None, ("energy", "slab", "row"), None),
        check_vma=False,
    )
```

profile of v0, /device:TPU:0, one launch (start us, length us, event | category | flops | bytes accessed | tf_op | source)
XLA Modules:
  0.0 169.6 jit_solution(9817298813051261723)
XLA Ops:
  6.5 5.0 %collective-permute-start = (bf16[2,128,128]{2,1,0:T(8,128)(2,1)}, bf16[2,128,128]{2,1,0:T(8,128)(2,1)S(1)}, u32[]{:S(2)}, u32[]{:S(2)}) collective-permute-start(bf16[2,128,128]{2,1,0:T(8,128)(2,1)} %param.9), channel_id=1, source_target_pairs={{0,2},{2,4},{4,6},{6,8},{8,10},{10,12},{12,14},{1,3},{3,5},{5,7},{... | collective-permute-start | bytes 196616 | tf_op jit(solution)/shard_map/ppermute | solution.py:10
  12.2 1.1 copy.7
  13.4 2.1 %all_gather.39 = bf16[2,768,128]{1,2,0:T(8,128)(2,1)S(1)} all-gather(bf16[2,384,128]{1,2,0:T(8,128)(2,1)S(1)} %multiply_convert_fusion), channel_id=1, replica_groups=mesh['energy'=2,'slab'=8,'row'=2] {'row'}, dimensions={1}, use_global_device_ids=true | all-gather | bytes 589824 | tf_op jit(solution)/shard_map/all_gather | solution.py:62
  15.5 2.0 %all_gather.40 = bf16[2,256,256]{2,1,0:T(8,128)(2,1)S(1)} all-gather(bf16[2,128,256]{2,1,0:T(8,128)(2,1)S(1)} %pad_maximum_fusion.1), channel_id=1, replica_groups=mesh['energy'=2,'slab'=8,'row'=2] {'row'}, dimensions={1}, use_global_device_ids=true | all-gather | bytes 393216 | tf_op jit(solution)/shard_map/all_gather | solution.py:70
  18.2 0.7 pad_maximum_fusion.2
  19.0 0.3 fusion.52
  19.3 0.3 fusion.33
  19.6 0.3 fusion.50
  20.0 0.3 fusion.32
  20.3 1.9 %all_gather.43 = bf16[2,256,128]{1,2,0:T(8,128)(2,1)S(1)} all-gather(bf16[2,128,128]{1,2,0:T(8,128)(2,1)S(1)} %fusion.62), channel_id=1, replica_groups=mesh['energy'=2,'slab'=8,'row'=2] {'row'}, dimensions={1}, use_global_device_ids=true | all-gather | bytes 196608 | tf_op jit(solution)/shard_map/all_gather | solution.py:73
  22.2 1.3 collective-permute-start.1
  24.3 0.7 pad_maximum_fusion.3
  25.0 3.4 %collective-permute-done.1 = bf16[2,128,128]{1,2,0:T(8,128)(2,1)S(1)} collective-permute-done((bf16[2,128,128]{1,2,0:T(8,128)(2,1)S(1)}, bf16[2,128,128]{1,2,0:T(8,128)(2,1)S(1)}, u32[]{:S(2)}, u32[]{:S(2)}) %collective-permute-start.1) | collective-permute-done | bytes 65568 | tf_op jit(solution)/shard_map/ppermute | solution.py:10
  29.7 0.2 fusion.42
  30.3 32.5 %all-gather.1 = f32[16,128,64]{1,2,0:T(8,128)S(1)} all-gather(f32[2,128,64]{1,2,0:T(8,128)S(1)} %fusion.86), channel_id=3, replica_groups=mesh['energy'=2,'slab'=8,'row'=2] {'slab'}, dimensions={0}, use_global_device_ids=true | all-gather | bytes 589824 | tf_op jit(solution)/shard_map/all_gather | solution.py:17
  62.8 1.9 %all_gather.46 = bf16[2,128,128]{1,2,0:T(8,128)(2,1)S(1)} all-gather(bf16[2,128,64]{1,2,0:T(8,128)(2,1)S(1)} %convert_element_type.52), channel_id=1, replica_groups=mesh['energy'=2,'slab'=8,'row'=2] {'row'}, dimensions={2}, use_global_device_ids=true | all-gather | bytes 98304 | tf_op jit(solution)/shard_map/all_gather | solution.py:102
  66.2 60.2 %all-gather.3 = f32[16,128,64]{1,2,0:T(8,128)S(1)} all-gather(f32[2,128,64]{1,2,0:T(8,128)S(1)} %fusion.84), channel_id=5, replica_groups=mesh['energy'=2,'slab'=8,'row'=2] {'slab'}, dimensions={0}, use_global_device_ids=true | all-gather | bytes 589824 | tf_op jit(solution)/shard_map/all_gather | solution.py:17
  126.5 30.9 %while.27 = (s32[]{:T(128)}, f32[2,128,64]{1,2,0:T(8,128)S(1)}, s32[]{:T(128)}, f32[8,2,128,128]{3,2,1,0:T(8,128)}, f32[8,2,128,64]{2,3,1,0:T(8,128)S(1)}, /*ind...) while((s32[]{:T(128)}, f32[2,128,64]{1,2,0:T(8,128)S(1)}, s32[]{:T(128)}, f32[8,2,128,128]{3,2,1,0:T(8,128)}, ...), condition=%wide.region_3.4_spmd, body=%wide.region_2.3_spmd.sunk | while | flops 50380808 | bytes 786619 | solution.py:26
  126.5 1.1 fusion.160
  127.6 1.1 fusion.161
  128.7 1.1 fusion.158
  129.8 1.1 fusion.159
  130.9 1.1 fusion.160
  132.0 1.1 fusion.161
  133.1 1.1 fusion.158
  134.2 1.1 fusion.159
  135.3 1.1 fusion.160
  136.4 1.1 fusion.161
  137.5 1.1 fusion.158
  138.6 1.1 fusion.159
  139.7 1.1 fusion.160
  140.8 1.1 fusion.161
  141.9 1.1 fusion.158
  143.0 1.1 fusion.159
  144.2 1.1 fusion.160
  145.2 1.1 fusion.161
  146.3 1.1 fusion.158
  147.4 1.1 fusion.159
  148.6 1.1 fusion.160
  149.7 1.1 fusion.161
  150.8 1.1 fusion.158
  151.8 1.1 fusion.159
  153.0 1.1 fusion.160
  154.1 1.1 fusion.161
  155.2 1.1 fusion.158
  156.3 1.1 fusion.159
  157.4 1.9 %all_gather.51 = bf16[2,128,128]{1,2,0:T(8,128)(2,1)S(1)} all-gather(bf16[2,128,64]{1,2,0:T(8,128)(2,1)S(1)} %convert_element_type.53), channel_id=1, replica_groups=mesh['energy'=2,'slab'=8,'row'=2] {'row'}, dimensions={2}, use_global_device_ids=true | all-gather | bytes 98304 | tf_op jit(solution)/shard_map/all_gather | solution.py:112
  161.8 0.9 copy.8
  (69 shorter events, 7.4 us)
Async XLA Ops:
  6.5 8.9 %copy-start = (bf16[2,384,768]{2,1,0:T(8,128)(2,1)S(1)}, bf16[2,384,768]{2,1,0:T(8,128)(2,1)}, u32[]{:S(2)}) copy-start(bf16[2,384,768]{2,1,0:T(8,128)(2,1)} %param.8) | copy-start | bytes 3538948
  6.5 56.3 %all-gather.7.cloned.1.call-start = ((), (), s32[]{:S(2)}) async-start(), calls=%async_computation | async-start | bytes 1179648 | tf_op jit(solution)/shard_map/all_gather | solution.py:17
  6.5 11.0 %collective-permute-start = (bf16[2,128,128]{2,1,0:T(8,128)(2,1)}, bf16[2,128,128]{2,1,0:T(8,128)(2,1)S(1)}, u32[]{:S(2)}, u32[]{:S(2)}) collective-permute-start(bf16[2,128,128]{2,1,0:T(8,128)(2,1)} %param.9), channel_id=1, source_target_pairs={{0,2},{2,4},{4,6},{6,8},{8,10},{10,12},{12,14},{1,3},{3,5},{5,7},{... | collective-permute-start | bytes 196616 | tf_op jit(solution)/shard_map/ppermute | solution.py:10
  18.9 107.5 %all-gather.9.cloned.1.call-start = ((), (), s32[]{:S(2)}) async-start(), calls=%async_computation.1 | async-start | bytes 1179648 | tf_op jit(solution)/shard_map/all_gather | solution.py:17
  19.9 3.6 %copy-start.1 = (bf16[2,128,128]{2,1,0:T(8,128)(2,1)S(1)}, bf16[2,128,128]{2,1,0:T(8,128)(2,1)}, u32[]{:S(2)}) copy-start(bf16[2,128,128]{2,1,0:T(8,128)(2,1)} %param.9) | copy-start | bytes 196612
  22.2 6.2 %collective-permute-start.1 = (bf16[2,128,128]{1,2,0:T(8,128)(2,1)S(1)}, bf16[2,128,128]{1,2,0:T(8,128)(2,1)S(1)}, u32[]{:S(2)}, u32[]{:S(2)}) collective-permute-start(bf16[2,128,128]{1,2,0:T(8,128)(2,1)S(1)} %slice.453), channel_id=1, source_target_pairs={{2,0},{4,2},{6,4},{8,6},{10,8},{12,10},{14,12},{3,1},{5,3},{7,5},{... | collective-permute-start | bytes 196616 | tf_op jit(solution)/shard_map/ppermute | solution.py:10
Sparse Core Ops, SparseCore 0:
  19.1 43.7 all-gather.6
  64.9 39.1 all-gather.8
where the time goes:
time: 171 us; the launch traced here: 170 us
  blocking collectives  102 us (60%)
  matrix products  38.8 us (23%)
  between operations  14.5 us (8%)
  starting transfers between devices  6.33 us (4%)
  waiting for transfers between devices  3.47 us (2%)
  local copies, waits for them, and re-layouts  2.07 us (1%)
    all_gather x2, blocking collectives, carried_in(): gathered = jax.tree.map(lambda a: lax.all_gather(a, axis), part)  92.7 us
    dot_general x68, matrix products, multiply(): jnp.dot(matrix, operand, preferred_element_type=jnp.float32, precision=la...  38.8 us
    ppermute x2, starting transfers between devices, passed_along(): return lax.ppermute(block, axis, route)  6.28 us
  transfers between devices with their start and end apart: 4, of which 2 were waited for; matrix products, arithmetic and copies ran while one was open for 4% of the time, Pallas kernels for 0%

commit v1 on v0

v1 whole, which is shorter than its diff:
```python
import functools

import jax
import jax.numpy as jnp
from jax import lax
from jax.experimental import pallas as pl
from jax.experimental.pallas import tpu as pltpu
from jax.sharding import PartitionSpec as P

F32 = jnp.float32
BF16 = jnp.bfloat16

SOURCE, COUPLE, EDGE, MAP_A, TERM_A, BACK_B, CROSS_B, FIRST_B, STATE, LOWER, AFTER, UPPER = range(12)
(S_SOURCE, S_COUPLE, S_EDGE, S_0, S_1, S_2, S_3, S_LOWER, S_UPPER) = range(9)


def dot(a, b):
    return jnp.dot(a, b, preferred_element_type=F32)


def embed(real, imag):
    return jnp.concatenate(
        [jnp.concatenate([real, -imag], axis=1), jnp.concatenate([imag, real], axis=1)], axis=0
    )


def halves(x):
    high = x.astype(BF16)
    return high, (x - high.astype(F32)).astype(BF16)


def wide_map(x):
    w = x.shape[0] // 2
    high, low = halves(x)
    return embed(high[:w], high[w:]), embed(low[:w], low[w:])


def apply_exact(matrix, x):
    c = x.shape[1]
    y = dot(matrix, jnp.concatenate(halves(x), axis=1))
    return y[:, :c] + y[:, c:]


def apply_wide(matrix, x):
    c = x.shape[1]
    high, low = halves(x)
    y = dot(matrix[0], jnp.concatenate([high, low], axis=1))
    return y[:, :c] + (y[:, c:] + dot(matrix[1], high))


def kernel(
    count, green_hbm, couple_hbm, source_hbm, interior_ref, out_ref,
    green, couple, source, source_in, couple_in, edge_in, map_a, term_a, back_b, cross_b, first_b,
    state, lower, after, upper, edge_out, out_0, out_1, out_2, low_out, up_out,
    copy_sem, send_sem, recv_sem,
):
    rows, width = green.shape[1], green.shape[2]
    w = couple.shape[1]
    cols = source.shape[2]
    s = lax.axis_index("slab")
    r = lax.axis_index("row")
    odd = lax.rem(s, 2)
    pair = s // 2
    pairs = count // 2

    loads = [
        pltpu.make_async_copy(source_hbm, source, copy_sem.at[0]),
        pltpu.make_async_copy(green_hbm, green, copy_sem.at[1]),
        pltpu.make_async_copy(couple_hbm, couple, copy_sem.at[2]),
    ]
    for load in loads:
        load.start()

    buffers = [source_in, couple_in, edge_in, map_a, term_a, back_b, cross_b, first_b, state, lower, after, upper]

    def push(src, slot, out_slot, slab, row):
        copy = pltpu.make_async_remote_copy(
            src_ref=src, dst_ref=buffers[slot], send_sem=send_sem.at[out_slot], recv_sem=recv_sem.at[slot],
            device_id={"slab": slab, "row": row}, device_id_type=pl.DeviceIdType.MESH,
        )
        copy.start()
        return copy

    def arrived(slot):
        pltpu.make_async_remote_copy(
            src_ref=buffers[slot], dst_ref=buffers[slot], send_sem=send_sem.at[0], recv_sem=recv_sem.at[slot],
            device_id={"slab": s, "row": 1 - r}, device_id_type=pl.DeviceIdType.MESH,
        ).wait_recv()

    def sent(src, out_slot):
        pltpu.make_async_remote_copy(
            src_ref=src, dst_ref=src, send_sem=send_sem.at[out_slot], recv_sem=recv_sem.at[0],
            device_id={"slab": s, "row": 1 - r}, device_id_type=pl.DeviceIdType.MESH,
        ).wait_send()

    barrier = pltpu.get_barrier_semaphore()
    leader = jnp.logical_or(jnp.logical_and(odd == 0, r == 0), jnp.logical_and(odd == 1, r == 1))
    side = jnp.where(r == 1, s + 1, s - 1)
    partners = [
        (s, 1 - r, None),
        (s - 1, r, s > 0),
        (s + 1, r, s < count - 1),
        (side, 1 - r, jnp.logical_and(side >= 0, side < count)),
        (s - 2, r, jnp.logical_and(leader, s >= 2)),
        (s + 2, r, jnp.logical_and(leader, s < count - 2)),
    ]
    expected = 1
    for slab, row, there in partners:
        def greet(slab=slab, row=row):
            pl.semaphore_signal(
                barrier, inc=1, device_id={"slab": slab, "row": row}, device_id_type=pl.DeviceIdType.MESH
            )
        if there is None:
            greet()
        else:
            pl.when(there)(greet)
            expected = expected + there.astype(jnp.int32)
    pl.semaphore_wait(barrier, expected)

    push(source_hbm, SOURCE, S_SOURCE, s, 1 - r)

    @pl.when(s < count - 1)
    def _():
        push(couple_hbm, COUPLE, S_COUPLE, s + 1, r)

    interior = interior_ref[0]

    def injected(ref, half):
        orbital = half * rows + lax.broadcasted_iota(jnp.int32, (rows, cols), 0)
        live = jnp.logical_or(orbital < w + interior, orbital >= width - w).astype(F32)
        return jnp.concatenate(
            [(ref[0].astype(F32) * live).astype(BF16), (ref[1].astype(F32) * live).astype(BF16)], axis=1
        )

    def add_product(x, columns, first):
        by_real = dot(green[0, :, columns], x)
        by_imag = dot(green[1, :, columns], x)
        real = by_real[:, :cols] - by_imag[:, cols:]
        imag = by_real[:, cols:] + by_imag[:, :cols]
        if first:
            out_ref[0], out_ref[1] = real, imag
        else:
            out_ref[0] += real
            out_ref[1] += imag

    loads[0].wait()
    loads[1].wait()
    add_product(injected(source, r), pl.ds(pl.multiple_of(r * rows, w), rows), True)
    arrived(SOURCE)
    add_product(injected(source_in, 1 - r), pl.ds(pl.multiple_of((1 - r) * rows, w), rows), False)

    loads[2].wait()
    head, tail = slice(0, w), slice(width - w, width)
    has_next = (s < count - 1).astype(F32)

    def next_coupling():
        return (couple[...].astype(F32) * has_next).astype(BF16).reshape(2 * w, w)

    def previous_coupling():
        @pl.when(s > 0)
        def _():
            arrived(COUPLE)

        @pl.when(s == 0)
        def _():
            couple_in[...] = jnp.zeros_like(couple_in)

    def previous_adjoint():
        return (
            couple_in[0].astype(F32).T.astype(BF16),
            (-couple_in[1].astype(F32).T).astype(BF16),
        )

    def block(first_row, columns):
        return embed(
            green[0, first_row:first_row + w, columns], green[1, first_row:first_row + w, columns]
        )

    def surface(first_row):
        return jnp.concatenate(
            [out_ref[0, first_row:first_row + w, :], out_ref[1, first_row:first_row + w, :]], axis=0
        )

    def pairwise(ref):
        return jnp.concatenate([ref[:w], ref[w:]], axis=1)

    def no_state(ref, there, slot):
        @pl.when(there)
        def _():
            arrived(slot)

        @pl.when(jnp.logical_not(there))
        def _():
            ref[...] = jnp.zeros_like(ref)

    def row_zero(even):
        first = surface(0)
        edge_out[...] = first.astype(BF16)

        @pl.when(s > 0)
        def _():
            push(edge_out, EDGE, S_EDGE, s - 1, 1)

        if not even:
            out_0[...] = first
            push(out_0, FIRST_B, S_0, s - 1, 0)
        couple_now = next_coupling()
        back = dot(block(0, tail), couple_now)
        if not even:
            out_1[...] = back
            push(out_1, BACK_B, S_1, s - 1, 0)
        previous_coupling()
        adj_real, adj_imag = previous_adjoint()
        adjoint = embed(adj_real, adj_imag)
        cross = dot(block(0, head), jnp.concatenate([adj_real, adj_imag], axis=0))
        if not even:
            out_2[...] = cross
            push(out_2, CROSS_B, S_2, s - 1, 0)
            couple_map = embed(couple_now[:w], couple_now[w:])
            arrived(STATE)
        else:
            couple_map = embed(couple_now[:w], couple_now[w:])
            arrived(BACK_B)
            back_own = wide_map(back)
            back_two = wide_map(apply_wide(back_own, back_b[...]))
            back_far = wide_map(back_b[...])
            arrived(CROSS_B)
            arrived(MAP_A)
            cross_far = wide_map(cross_b[...])
            cross_two_f = apply_wide(cross_far, map_a[...])
            cross_two = wide_map(cross_two_f)
            cross_all = wide_map(cross + apply_wide(back_own, cross_two_f))
            arrived(FIRST_B)
            arrived(TERM_A)
            term_b = first_b[...] + apply_wide(cross_far, term_a[...])
            term = first + apply_wide(back_own, term_b)
            no_state(state, pair > 0, STATE)
            before = state[...]
            term = term + apply_wide(cross_all, before)
            no_state(after, pair < pairs - 1, AFTER)
            follow = after[...]
            out_0[...] = term + apply_wide(back_two, follow)

            @pl.when(pair > 0)
            def _():
                push(out_0, AFTER, S_0, s - 2, 0)
                push(out_0, AFTER, S_1, s - 1, 0)

            after_own = term_b + apply_wide(cross_two, before) + apply_wide(back_far, follow)
        low_out[...] = apply_exact(adjoint, state[...]).astype(BF16)
        push(low_out, LOWER, S_LOWER, s, 1)
        if even:
            up_out[...] = apply_exact(couple_map, after_own).astype(BF16)
            push(up_out, UPPER, S_UPPER, s, 1)
            add_product(pairwise(low_out), head, False)
            add_product(pairwise(up_out), tail, False)
        else:
            add_product(pairwise(low_out), head, False)
            no_state(after, pair < pairs - 1, AFTER)
            up_out[...] = apply_exact(couple_map, after[...]).astype(BF16)
            push(up_out, UPPER, S_UPPER, s, 1)
            add_product(pairwise(up_out), tail, False)
        sent(low_out, S_LOWER)
        sent(up_out, S_UPPER)

        @pl.when(s > 0)
        def _():
            sent(edge_out, S_EDGE)

        if even:
            @pl.when(pair > 0)
            def _():
                sent(out_0, S_0)
                sent(out_0, S_1)
        else:
            sent(out_0, S_0)
            sent(out_1, S_1)
            sent(out_2, S_2)

    def row_one(even):
        last = surface(rows - w)
        previous_coupling()
        adj_real, adj_imag = previous_adjoint()
        forward = dot(block(rows - w, head), jnp.concatenate([adj_real, adj_imag], axis=0))
        if even:
            out_0[...] = forward
            push(out_0, MAP_A, S_0, s, 0)
            push(out_0, MAP_A, S_1, s + 1, 1)
        else:
            own = wide_map(forward)
        turned = wide_map(dot(block(rows - w, tail), next_coupling()))
        if even:
            arrived(EDGE)
            edge = edge_in[...]
        else:
            no_state(edge_in, s < count - 1, EDGE)
            edge = edge_in[...]
        term = last + dot(turned[0], edge) + dot(turned[1], edge)
        if even:
            out_1[...] = term
            push(out_1, TERM_A, S_2, s + 1, 1)
            push(out_1, TERM_A, S_3, s, 0)
        else:
            arrived(MAP_A)
            both = wide_map(apply_wide(own, map_a[...]))
            near = wide_map(map_a[...])
            arrived(TERM_A)
            total = term + apply_wide(own, term_a[...])
            no_state(state, pair > 0, STATE)
            before = state[...]

            @pl.when(pair < pairs - 1)
            def _():
                out_0[...] = total + apply_wide(both, before)

                @pl.when(pair == pairs - 2)
                def _():
                    push(out_0, STATE, S_0, s + 1, 0)
                    push(out_0, STATE, S_1, s + 2, 1)

                @pl.when(pair < pairs - 2)
                def _():
                    push(out_0, STATE, S_1, s + 2, 1)
                    push(out_0, STATE, S_0, s + 1, 0)

            out_1[...] = term_a[...] + apply_wide(near, before)
            push(out_1, STATE, S_2, s, 0)
        arrived(LOWER)
        add_product(pairwise(lower), head, False)
        arrived(UPPER)
        add_product(pairwise(upper), tail, False)
        if even:
            sent(out_0, S_0)
            sent(out_0, S_1)
            sent(out_1, S_2)
            sent(out_1, S_3)
        else:
            @pl.when(pair < pairs - 1)
            def _():
                sent(out_0, S_0)
                sent(out_0, S_1)

            sent(out_1, S_2)

    for row, role in ((0, row_zero), (1, row_one)):
        for parity in (0, 1):
            @pl.when(jnp.logical_and(r == row, odd == parity))
            def _(role=role, parity=parity):
                role(parity == 0)

    sent(source_hbm, S_SOURCE)

    @pl.when(s < count - 1)
    def _():
        sent(couple_hbm, S_COUPLE)


def body(green_blocks, coupling, source, interior_count):
    rows, width = green_blocks.shape[1:]
    w = coupling.shape[1]
    cols = source.shape[2]
    block = pltpu.VMEM((2 * w, cols), F32)
    small = pltpu.VMEM((2 * w, cols), BF16)
    square = pltpu.VMEM((2 * w, w), F32)
    result = pl.pallas_call(
        functools.partial(kernel, lax.axis_size("slab")),
        out_shape=jax.ShapeDtypeStruct((2, rows, cols), F32),
        in_specs=[pl.BlockSpec(memory_space=pl.ANY)] * 3 + [pl.BlockSpec(memory_space=pltpu.SMEM)],
        out_specs=pl.BlockSpec(memory_space=pltpu.VMEM),
        scratch_shapes=[
            pltpu.VMEM(green_blocks.shape, BF16),
            pltpu.VMEM(coupling.shape, BF16),
            pltpu.VMEM(source.shape, BF16),
            pltpu.VMEM(source.shape, BF16),
            pltpu.VMEM(coupling.shape, BF16),
            small,
            square,
            block,
            square,
            square,
            block,
            block,
            small,
            block,
            small,
            small,
            block,
            block,
            square,
            small,
            small,
            pltpu.SemaphoreType.DMA((3,)),
            pltpu.SemaphoreType.DMA((9,)),
            pltpu.SemaphoreType.DMA((12,)),
        ],
        compiler_params=pltpu.CompilerParams(
            collective_id=0, has_side_effects=True, vmem_limit_bytes=32 * 1024 * 1024
        ),
    )(green_blocks, coupling, source, interior_count)
    orbital = lax.axis_index("row") * rows + lax.iota(jnp.int32, rows)
    live = ((orbital < w + interior_count[0]) | (orbital >= width - w)).astype(F32)
    return result * live[None, :, None]


def solution(mesh):
    placed = (
        P(None, ("energy", "slab", "row"), None),
        P(None, "slab", None),
        P(None, ("energy", "slab", "row"), None),
        P("slab"),
    )
    return jax.shard_map(
        body,
        mesh=mesh,
        in_specs=placed,
        out_specs=P(None, ("energy", "slab", "row"), None),
        check_vma=False,
    )
```

time: 171 us -> 42.3 us (0.25)
  the two profiles are of different devices: /device:TPU:0 before, /device:TPU:5 now
where the time goes in v1:
time: 42.3 us; the launch traced here: 42.1 us
  Pallas kernels  37.5 us (89%)
  local copies, waits for them, and re-layouts  3.03 us (7%)
  other arithmetic  0.87 us (2%)
  between operations  0.68 us (2%)
    pallas_call x1, Pallas kernels, body(): pl.pallas_call(functools.partial(kernel, lax.axis_size('slab')), out_shap...  37.5 us
    unnamed x6, local copies, waits for them, and re-layouts  3.03 us
    mul x1, other arithmetic, body(): return result * live[None, :, None]  0.87 us

profile of v1, /device:TPU:5, one launch (start us, length us, event | category | flops | bytes accessed | tf_op | source)
XLA Modules:
  0.0 42.1 jit_solution(10099095675031774175)
XLA Ops:
  0.7 0.0 copy-start
  0.7 1.3 %copy-done = bf16[2,384,768]{2,1,0:T(8,128)(2,1)S(1)} copy-done((bf16[2,384,768]{2,1,0:T(8,128)(2,1)S(1)}, bf16[2,384,768]{2,1,0:T(8,128)(2,1)}, u32[]{:S(2)}) %copy-start) | copy-done | bytes 1179672
  1.9 0.0 copy-start.1
  1.9 0.9 %copy-done.1 = bf16[2,384,128]{2,1,0:T(8,128)(2,1)S(1)} copy-done((bf16[2,384,128]{2,1,0:T(8,128)(2,1)S(1)}, bf16[2,384,128]{2,1,0:T(8,128)(2,1)}, u32[]{:S(2)}) %copy-start.1) | copy-done | bytes 196632
  2.9 0.0 copy-start.2
  2.9 0.8 %copy-done.2 = bf16[2,128,128]{2,1,0:T(8,128)(2,1)S(1)} copy-done((bf16[2,128,128]{2,1,0:T(8,128)(2,1)S(1)}, bf16[2,128,128]{2,1,0:T(8,128)(2,1)}, u32[]{:S(2)}) %copy-start.2) | copy-done | bytes 65560
  3.7 37.5 %shard_map.46 = f32[2,384,128]{2,1,0:T(8,128)S(1)} custom-call(bf16[2,384,768]{2,1,0:T(8,128)(2,1)S(1)} %copy-done, bf16[2,128,128]{2,1,0:T(8,128)(2,1)S(1)} %copy-done.2, bf16[2,384,128]{2,1,0:T(8,128)(2,1)S(1)} %copy-done.1, s32[1]{0:T(128)S(6)} %copy.5.interior_ref), custom_call_target="tpu_custom_call" | custom-call | tf_op jit(solution)/shard_map/pallas_call | solution.py:365
  41.3 0.9 %broadcast_multiply_fusion = f32[2,384,128]{2,1,0:T(8,128)} fusion(f32[2,384,128]{2,1,0:T(8,128)S(1)} %shard_map.46, f32[384]{0:T(512)S(1)} %fusion.3), kind=kLoop, calls=%fused_computation | loop fusion | flops 98304 | bytes 787968 | tf_op jit(solution)/shard_map/mul | solution.py:402
  (1 shorter events, 0.0 us)
Async XLA Ops:
  0.7 1.3 %copy-start = (bf16[2,384,768]{2,1,0:T(8,128)(2,1)S(1)}, bf16[2,384,768]{2,1,0:T(8,128)(2,1)}, u32[]{:S(2)}) copy-start(bf16[2,384,768]{2,1,0:T(8,128)(2,1)} %green_hbm.1) | copy-start | bytes 3538948
  1.9 0.9 %copy-start.1 = (bf16[2,384,128]{2,1,0:T(8,128)(2,1)S(1)}, bf16[2,384,128]{2,1,0:T(8,128)(2,1)}, u32[]{:S(2)}) copy-start(bf16[2,384,128]{2,1,0:T(8,128)(2,1)} %source_hbm.1) | copy-start | bytes 589828
  2.9 0.8 %copy-start.2 = (bf16[2,128,128]{2,1,0:T(8,128)(2,1)S(1)}, bf16[2,128,128]{2,1,0:T(8,128)(2,1)}, u32[]{:S(2)}) copy-start(bf16[2,128,128]{2,1,0:T(8,128)(2,1)} %couple_hbm.1) | copy-start | bytes 196612

commit v2 on v1

--- a/solution.py
+++ b/solution.py
@@ -48,10 +48,14 @@
     return y[:, :c] + (y[:, c:] + dot(matrix[1], high))
 
 
+def apply_rounded(matrix, x):
+    return dot(matrix[0], x) + dot(matrix[1], x)
+
+
 def kernel(
     count, green_hbm, couple_hbm, source_hbm, interior_ref, out_ref,
     green, couple, source, source_in, couple_in, edge_in, map_a, term_a, back_b, cross_b, first_b,
-    state, lower, after, upper, edge_out, out_0, out_1, out_2, low_out, up_out,
+    state, lower, after, upper, edge_out, out_0, out_1, out_2, ship, low_out, up_out,
     copy_sem, send_sem, recv_sem,
 ):
     rows, width = green.shape[1], green.shape[2]
@@ -103,6 +107,7 @@
         (side, 1 - r, jnp.logical_and(side >= 0, side < count)),
         (s - 2, r, jnp.logical_and(leader, s >= 2)),
         (s + 2, r, jnp.logical_and(leader, s < count - 2)),
+        (jnp.where(odd == 1, s - 1, s + 1), 1 - r, leader),
     ]
     expected = 1
     for slab, row, there in partners:
@@ -217,7 +222,6 @@
             out_2[...] = cross
             push(out_2, CROSS_B, S_2, s - 1, 0)
             couple_map = embed(couple_now[:w], couple_now[w:])
-            arrived(STATE)
         else:
             couple_map = embed(couple_now[:w], couple_now[w:])
             arrived(BACK_B)
@@ -232,35 +236,46 @@
             cross_all = wide_map(cross + apply_wide(back_own, cross_two_f))
             arrived(FIRST_B)
             arrived(TERM_A)
-            term_b = first_b[...] + apply_wide(cross_far, term_a[...])
+            term_b = first_b[...] + apply_rounded(cross_far, term_a[...])
             term = first + apply_wide(back_own, term_b)
             no_state(state, pair > 0, STATE)
             before = state[...]
-            term = term + apply_wide(cross_all, before)
+            term = term + apply_rounded(cross_all, before)
+
+            @pl.when(pair == pairs - 1)
+            def _():
+                ship[...] = term.astype(BF16)
+                push(ship, AFTER, S_0, s - 2, 0)
+                push(state, STATE, S_2, s + 1, 1)
+
+            low_out[...] = dot(adjoint, before).astype(BF16)
+            push(low_out, LOWER, S_LOWER, s, 1)
+            after_own = term_b + apply_rounded(cross_two, before)
+            add_product(pairwise(low_out), head, False)
             no_state(after, pair < pairs - 1, AFTER)
             follow = after[...]
-            out_0[...] = term + apply_wide(back_two, follow)
-
-            @pl.when(pair > 0)
-            def _():
-                push(out_0, AFTER, S_0, s - 2, 0)
-                push(out_0, AFTER, S_1, s - 1, 0)
-
-            after_own = term_b + apply_wide(cross_two, before) + apply_wide(back_far, follow)
-        low_out[...] = apply_exact(adjoint, state[...]).astype(BF16)
-        push(low_out, LOWER, S_LOWER, s, 1)
-        if even:
-            up_out[...] = apply_exact(couple_map, after_own).astype(BF16)
-            push(up_out, UPPER, S_UPPER, s, 1)
-            add_product(pairwise(low_out), head, False)
-            add_product(pairwise(up_out), tail, False)
-        else:
-            add_product(pairwise(low_out), head, False)
-            no_state(after, pair < pairs - 1, AFTER)
-            up_out[...] = apply_exact(couple_map, after[...]).astype(BF16)
+
+            @pl.when(jnp.logical_and(pair > 0, pair < pairs - 1))
+            def _():
+                ship[...] = (term + apply_rounded(back_two, follow)).astype(BF16)
+                push(ship, AFTER, S_0, s - 2, 0)
+                push(after, AFTER, S_2, s + 1, 0)
+
+            @pl.when(pair == 1)
+            def _():
+                push(ship, AFTER, S_1, s - 1, 0)
+
+            up_out[...] = apply_exact(couple_map, after_own + apply_rounded(back_far, follow)).astype(BF16)
             push(up_out, UPPER, S_UPPER, s, 1)
             add_product(pairwise(up_out), tail, False)
-        sent(low_out, S_LOWER)
+            sent(low_out, S_LOWER)
+        if not even:
+            arrived(LOWER)
+            add_product(pairwise(lower), head, False)
+            no_state(after, pair < pairs - 1, AFTER)
+            up_out[...] = dot(couple_map, after[...]).astype(BF16)
+            push(up_out, UPPER, S_UPPER, s, 1)
+            add_product(pairwise(up_out), tail, False)
         sent(up_out, S_UPPER)
 
         @pl.when(s > 0)
@@ -270,8 +285,12 @@
         if even:
             @pl.when(pair > 0)
             def _():
-                sent(out_0, S_0)
-                sent(out_0, S_1)
+                sent(ship, S_0)
+                sent(ship, S_2)
+
+            @pl.when(pair == 1)
+            def _():
+                sent(ship, S_1)
         else:
             sent(out_0, S_0)
             sent(out_1, S_1)
@@ -297,50 +316,58 @@
             edge = edge_in[...]
         term = last + dot(turned[0], edge) + dot(turned[1], edge)
         if even:
-            out_1[...] = term
-            push(out_1, TERM_A, S_2, s + 1, 1)
-            push(out_1, TERM_A, S_3, s, 0)
+            ship[...] = term.astype(BF16)
+            push(ship, TERM_A, S_2, s + 1, 1)
+            push(ship, TERM_A, S_3, s, 0)
         else:
             arrived(MAP_A)
             both = wide_map(apply_wide(own, map_a[...]))
             near = wide_map(map_a[...])
             arrived(TERM_A)
-            total = term + apply_wide(own, term_a[...])
+            total = term + apply_rounded(own, term_a[...])
             no_state(state, pair > 0, STATE)
             before = state[...]
 
             @pl.when(pair < pairs - 1)
             def _():
-                out_0[...] = total + apply_wide(both, before)
-
-                @pl.when(pair == pairs - 2)
-                def _():
-                    push(out_0, STATE, S_0, s + 1, 0)
-                    push(out_0, STATE, S_1, s + 2, 1)
-
-                @pl.when(pair < pairs - 2)
-                def _():
-                    push(out_0, STATE, S_1, s + 2, 1)
-                    push(out_0, STATE, S_0, s + 1, 0)
-
-            out_1[...] = term_a[...] + apply_wide(near, before)
-            push(out_1, STATE, S_2, s, 0)
-        arrived(LOWER)
-        add_product(pairwise(lower), head, False)
+                ship[...] = (total + apply_rounded(both, before)).astype(BF16)
+
+            @pl.when(pair == pairs - 2)
+            def _():
+                push(ship, STATE, S_0, s + 1, 0)
+
+            @pl.when(pair < pairs - 2)
+            def _():
+                push(ship, STATE, S_0, s + 2, 1)
+
+            @pl.when(jnp.logical_and(pair > 0, pair < pairs - 1))
+            def _():
+                push(state, STATE, S_1, s - 1, 0)
+
+            inner = term_a[...].astype(F32) + apply_rounded(near, before)
+            low_out[...] = apply_exact(embed(adj_real, adj_imag), inner).astype(BF16)
+            push(low_out, LOWER, S_LOWER, s, 0)
+            add_product(pairwise(low_out), head, False)
+        if even:
+            arrived(LOWER)
+            add_product(pairwise(lower), head, False)
         arrived(UPPER)
         add_product(pairwise(upper), tail, False)
         if even:
             sent(out_0, S_0)
             sent(out_0, S_1)
-            sent(out_1, S_2)
-            sent(out_1, S_3)
+            sent(ship, S_2)
+            sent(ship, S_3)
         else:
             @pl.when(pair < pairs - 1)
             def _():
-                sent(out_0, S_0)
-                sent(out_0, S_1)
-
-            sent(out_1, S_2)
+                sent(ship, S_0)
+
+            @pl.when(jnp.logical_and(pair > 0, pair < pairs - 1))
+            def _():
+                sent(state, S_1)
+
+            sent(low_out, S_LOWER)
 
     for row, role in ((0, row_zero), (1, row_one)):
         for parity in (0, 1):
@@ -365,7 +392,7 @@
     result = pl.pallas_call(
         functools.partial(kernel, lax.axis_size("slab")),
         out_shape=jax.ShapeDtypeStruct((2, rows, cols), F32),
-        in_specs=[pl.BlockSpec(memory_space=pl.ANY)] * 3 + [pl.BlockSpec(memory_space=pltpu.SMEM)],
+        in_specs=[pl.BlockSpec(memory_space=pltpu.HBM)] * 3 + [pl.BlockSpec(memory_space=pltpu.SMEM)],
         out_specs=pl.BlockSpec(memory_space=pltpu.VMEM),
         scratch_shapes=[
             pltpu.VMEM(green_blocks.shape, BF16),
@@ -375,18 +402,19 @@
             pltpu.VMEM(coupling.shape, BF16),
             small,
             square,
-            block,
+            small,
             square,
             square,
             block,
-            block,
-            small,
-            block,
+            small,
+            small,
+            small,
             small,
             small,
             block,
             block,
             square,
+            small,
             small,
             small,
             pltpu.SemaphoreType.DMA((3,)),
@@ -394,7 +422,7 @@
             pltpu.SemaphoreType.DMA((12,)),
         ],
         compiler_params=pltpu.CompilerParams(
-            collective_id=0, has_side_effects=True, vmem_limit_bytes=32 * 1024 * 1024
+            collective_id=0, has_side_effects=True, vmem_limit_bytes=60 * 1024 * 1024
         ),
     )(green_blocks, coupling, source, interior_count)
     orbital = lax.axis_index("row") * rows + lax.iota(jnp.int32, rows)

time: 42.3 us -> 35.2 us (0.83)
  Pallas kernels: 37.5 us -> 32.1 us
  local copies, waits for them, and re-layouts: 3.03 us -> 0 us
  other arithmetic: 0.87 us -> 1.87 us
    pallas_call x1, Pallas kernels: 37.5 us -> 32.1 us  [body(): pl.pallas_call(functools.partial(kernel, lax.axis_size('slab')), out_shap...]
    unnamed x6 -> x0, local copies, waits for them, and re-layouts: 3.03 us -> none
    mul x1, other arithmetic: 0.87 us -> 1.86 us  [body(): return result * live[None, :, None]]
where the time goes in v2:
time: 35.2 us; the launch traced here: 34.6 us
  Pallas kernels  32.1 us (91%)
  other arithmetic  1.87 us (5%)
  between operations  0.67 us (2%)
    pallas_call x1, Pallas kernels, body(): pl.pallas_call(functools.partial(kernel, lax.axis_size('slab')), out_shap...  32.1 us
    mul x1, other arithmetic, body(): return result * live[None, :, None]  1.86 us

profile of v2, /device:TPU:5, one launch (start us, length us, event | category | flops | bytes accessed | tf_op | source)
XLA Modules:
  0.0 34.6 jit_solution(3243210201192065424)
XLA Ops:
  0.7 32.1 %shard_map.46 = f32[2,384,128]{2,1,0:T(8,128)} custom-call(bf16[2,384,768]{2,1,0:T(8,128)(2,1)} %green_hbm.1, bf16[2,128,128]{2,1,0:T(8,128)(2,1)} %couple_hbm.1, bf16[2,384,128]{2,1,0:T(8,128)(2,1)} %source_hbm.1, s32[1]{0:T(128)S(6)} %copy.5.interior_ref), custom_call_target="tpu_custom_call" | custom-call | tf_op jit(solution)/shard_map/pallas_call | solution.py:392
  32.7 1.9 %broadcast_multiply_fusion = f32[2,384,128]{2,1,0:T(8,128)} fusion(f32[2,384,128]{2,1,0:T(8,128)} %shard_map.46, f32[384]{0:T(512)S(1)} %fusion.3), kind=kLoop, calls=%fused_computation | loop fusion | flops 98304 | bytes 787968 | tf_op jit(solution)/shard_map/mul | solution.py:430
  (1 shorter events, 0.0 us)

commit v3 on v2

--- a/solution.py
+++ b/solution.py
@@ -56,7 +56,8 @@
     count, green_hbm, couple_hbm, source_hbm, interior_ref, out_ref,
     green, couple, source, source_in, couple_in, edge_in, map_a, term_a, back_b, cross_b, first_b,
     state, lower, after, upper, edge_out, out_0, out_1, out_2, ship, low_out, up_out,
-    copy_sem, send_sem, recv_sem,
+    totals, total_maps, backs, back_maps, ship_map, running,
+    copy_sem, send_sem, recv_sem, far_send, far_recv,
 ):
     rows, width = green.shape[1], green.shape[2]
     w = couple.shape[1]
@@ -85,6 +86,55 @@
         copy.start()
         return copy
 
+    def far_copy(src, buffer, kind, place, q):
+        return pltpu.make_async_remote_copy(
+            src_ref=src, dst_ref=buffer.at[place], send_sem=far_send.at[kind % 2, q],
+            recv_sem=far_recv.at[kind, place],
+            device_id={"slab": 2 * q, "row": 0}, device_id_type=pl.DeviceIdType.MESH,
+        )
+
+    def far_push(src, buffer, kind, wanted):
+        order = range(pairs) if kind >= 2 else reversed(range(pairs))
+        for q in order:
+            pl.when(wanted(q))(lambda q=q: far_copy(src, buffer, kind, pair, q).start())
+
+    def far_sent(src, buffer, kind, wanted):
+        for q in range(pairs):
+            pl.when(wanted(q))(lambda q=q: far_copy(src, buffer, kind, pair, q).wait_send())
+
+    def far_arrived(buffer, kind, place):
+        far_copy(buffer.at[place], buffer, kind, place, 0).wait_recv()
+
+    def run(blocks, maps, kind, start, steps, stride):
+        running[...] = jnp.zeros_like(running)
+
+        def step(i, carry):
+            place = start + stride * i
+            far_arrived(blocks, kind, place)
+
+            @pl.when(i > 0)
+            def _():
+                far_arrived(maps, kind + 1, place)
+                matrix = maps[place]
+                running[...] = apply_exact(embed(matrix[:w], matrix[w:]), running[...])
+
+            running[...] += blocks[place].astype(F32)
+            return carry
+
+        lax.fori_loop(0, steps, step, 0)
+
+    def later_term(q):
+        return q > pair
+
+    def later_map(q):
+        return jnp.logical_and(pair > 0, q > pair)
+
+    def earlier_term(q):
+        return q < pair
+
+    def earlier_map(q):
+        return jnp.logical_and(pair < pairs - 1, q < pair)
+
     def arrived(slot):
         pltpu.make_async_remote_copy(
             src_ref=buffers[slot], dst_ref=buffers[slot], send_sem=send_sem.at[0], recv_sem=recv_sem.at[slot],
@@ -105,10 +155,14 @@
         (s - 1, r, s > 0),
         (s + 1, r, s < count - 1),
         (side, 1 - r, jnp.logical_and(side >= 0, side < count)),
-        (s - 2, r, jnp.logical_and(leader, s >= 2)),
-        (s + 2, r, jnp.logical_and(leader, s < count - 2)),
         (jnp.where(odd == 1, s - 1, s + 1), 1 - r, leader),
     ]
+    first_leader = jnp.logical_and(odd == 0, r == 0)
+    last_leader = jnp.logical_and(odd == 1, r == 1)
+    for q in range(pairs):
+        partners.append((2 * q, 0, jnp.logical_and(first_leader, pair != q)))
+        partners.append((2 * q + 1, 1, jnp.logical_and(first_leader, q < pair)))
+        partners.append((2 * q, 0, jnp.logical_and(last_leader, q > pair)))
     expected = 1
     for slab, row, there in partners:
         def greet(slab=slab, row=row):
@@ -226,7 +280,8 @@
             couple_map = embed(couple_now[:w], couple_now[w:])
             arrived(BACK_B)
             back_own = wide_map(back)
-            back_two = wide_map(apply_wide(back_own, back_b[...]))
+            ship_map[...] = apply_wide(back_own, back_b[...]).astype(BF16)
+            far_push(ship_map, back_maps, 3, earlier_map)
             back_far = wide_map(back_b[...])
             arrived(CROSS_B)
             arrived(MAP_A)
@@ -238,34 +293,29 @@
             arrived(TERM_A)
             term_b = first_b[...] + apply_rounded(cross_far, term_a[...])
             term = first + apply_wide(back_own, term_b)
-            no_state(state, pair > 0, STATE)
-            before = state[...]
-            term = term + apply_rounded(cross_all, before)
-
-            @pl.when(pair == pairs - 1)
+            run(totals, total_maps, 0, 0, pair, 1)
+            before = running[...]
+            ship[...] = (term + apply_wide(cross_all, before)).astype(BF16)
+            far_push(ship, backs, 2, earlier_term)
+
+            @pl.when(pair > 0)
             def _():
-                ship[...] = term.astype(BF16)
-                push(ship, AFTER, S_0, s - 2, 0)
+                state[...] = before.astype(BF16)
                 push(state, STATE, S_2, s + 1, 1)
 
-            low_out[...] = dot(adjoint, before).astype(BF16)
+            low_out[...] = apply_exact(adjoint, before).astype(BF16)
             push(low_out, LOWER, S_LOWER, s, 1)
-            after_own = term_b + apply_rounded(cross_two, before)
+            after_own = term_b + apply_wide(cross_two, before)
             add_product(pairwise(low_out), head, False)
-            no_state(after, pair < pairs - 1, AFTER)
-            follow = after[...]
-
-            @pl.when(jnp.logical_and(pair > 0, pair < pairs - 1))
+            run(backs, back_maps, 2, pairs - 1, pairs - 1 - pair, -1)
+            follow = running[...]
+
+            @pl.when(pair < pairs - 1)
             def _():
-                ship[...] = (term + apply_rounded(back_two, follow)).astype(BF16)
-                push(ship, AFTER, S_0, s - 2, 0)
-                push(after, AFTER, S_2, s + 1, 0)
-
-            @pl.when(pair == 1)
-            def _():
-                push(ship, AFTER, S_1, s - 1, 0)
-
-            up_out[...] = apply_exact(couple_map, after_own + apply_rounded(back_far, follow)).astype(BF16)
+                after[...] = follow.astype(BF16)
+                push(after, AFTER, S_0, s + 1, 0)
+
+            up_out[...] = apply_exact(couple_map, after_own + apply_wide(back_far, follow)).astype(BF16)
             push(up_out, UPPER, S_UPPER, s, 1)
             add_product(pairwise(up_out), tail, False)
             sent(low_out, S_LOWER)
@@ -285,12 +335,14 @@
         if even:
             @pl.when(pair > 0)
             def _():
-                sent(ship, S_0)
-                sent(ship, S_2)
-
-            @pl.when(pair == 1)
+                sent(state, S_2)
+
+            @pl.when(pair < pairs - 1)
             def _():
-                sent(ship, S_1)
+                sent(after, S_0)
+
+            far_sent(ship_map, back_maps, 3, earlier_map)
+            far_sent(ship, backs, 2, earlier_term)
         else:
             sent(out_0, S_0)
             sent(out_1, S_1)
@@ -321,29 +373,14 @@
             push(ship, TERM_A, S_3, s, 0)
         else:
             arrived(MAP_A)
-            both = wide_map(apply_wide(own, map_a[...]))
+            ship_map[...] = apply_wide(own, map_a[...]).astype(BF16)
+            far_push(ship_map, total_maps, 1, later_map)
             near = wide_map(map_a[...])
             arrived(TERM_A)
-            total = term + apply_rounded(own, term_a[...])
+            ship[...] = (term + apply_rounded(own, term_a[...])).astype(BF16)
+            far_push(ship, totals, 0, later_term)
             no_state(state, pair > 0, STATE)
             before = state[...]
-
-            @pl.when(pair < pairs - 1)
-            def _():
-                ship[...] = (total + apply_rounded(both, before)).astype(BF16)
-
-            @pl.when(pair == pairs - 2)
-            def _():
-                push(ship, STATE, S_0, s + 1, 0)
-
-            @pl.when(pair < pairs - 2)
-            def _():
-                push(ship, STATE, S_0, s + 2, 1)
-
-            @pl.when(jnp.logical_and(pair > 0, pair < pairs - 1))
-            def _():
-                push(state, STATE, S_1, s - 1, 0)
-
             inner = term_a[...].astype(F32) + apply_rounded(near, before)
             low_out[...] = apply_exact(embed(adj_real, adj_imag), inner).astype(BF16)
             push(low_out, LOWER, S_LOWER, s, 0)
@@ -359,14 +396,8 @@
             sent(ship, S_2)
             sent(ship, S_3)
         else:
-            @pl.when(pair < pairs - 1)
-            def _():
-                sent(ship, S_0)
-
-            @pl.when(jnp.logical_and(pair > 0, pair < pairs - 1))
-            def _():
-                sent(state, S_1)
-
+            far_sent(ship_map, total_maps, 1, later_map)
+            far_sent(ship, totals, 0, later_term)
             sent(low_out, S_LOWER)
 
     for row, role in ((0, row_zero), (1, row_one)):
@@ -389,6 +420,7 @@
     block = pltpu.VMEM((2 * w, cols), F32)
     small = pltpu.VMEM((2 * w, cols), BF16)
     square = pltpu.VMEM((2 * w, w), F32)
+    pairs = lax.axis_size("slab") // 2
     result = pl.pallas_call(
         functools.partial(kernel, lax.axis_size("slab")),
         out_shape=jax.ShapeDtypeStruct((2, rows, cols), F32),
@@ -417,9 +449,17 @@
             small,
             small,
             small,
+            pltpu.VMEM((pairs, 2 * w, cols), BF16),
+            pltpu.VMEM((pairs, 2 * w, w), BF16),
+            pltpu.VMEM((pairs, 2 * w, cols), BF16),
+            pltpu.VMEM((pairs, 2 * w, w), BF16),
+            pltpu.VMEM((2 * w, w), BF16),
+            block,
             pltpu.SemaphoreType.DMA((3,)),
             pltpu.SemaphoreType.DMA((9,)),
             pltpu.SemaphoreType.DMA((12,)),
+            pltpu.SemaphoreType.DMA((2, pairs)),
+            pltpu.SemaphoreType.DMA((4, pairs)),
         ],
         compiler_params=pltpu.CompilerParams(
             collective_id=0, has_side_effects=True, vmem_limit_bytes=60 * 1024 * 1024

time: 35.2 us -> 31.9 us (0.906); the launches traced: 34.6 us -> 31.8 us
  Pallas kernels: 32.1 us -> 29.2 us
    pallas_call x1, Pallas kernels: 32.1 us -> 29.2 us  [body(): pl.pallas_call(functools.partial(kernel, lax.axis_size('slab')), out_shap...]
where the time goes in v3:
time: 31.9 us; the launch traced here: 31.8 us
  Pallas kernels  29.2 us (92%)
  other arithmetic  1.87 us (6%)
  between operations  0.67 us (2%)
    pallas_call x1, Pallas kernels, body(): pl.pallas_call(functools.partial(kernel, lax.axis_size('slab')), out_shap...  29.2 us
    mul x1, other arithmetic, body(): return result * live[None, :, None]  1.86 us

profile of v3, /device:TPU:5, one launch (start us, length us, event | category | flops | bytes accessed | tf_op | source)
XLA Modules:
  0.0 31.8 jit_solution(10835288174135882516)
XLA Ops:
  0.7 29.2 %shard_map.46 = f32[2,384,128]{2,1,0:T(8,128)} custom-call(bf16[2,384,768]{2,1,0:T(8,128)(2,1)} %green_hbm.1, bf16[2,128,128]{2,1,0:T(8,128)(2,1)} %couple_hbm.1, bf16[2,384,128]{2,1,0:T(8,128)(2,1)} %source_hbm.1, s32[1]{0:T(128)S(6)} %copy.5.interior_ref), custom_call_target="tpu_custom_call" | custom-call | tf_op jit(solution)/shard_map/pallas_call | solution.py:424
  29.9 1.9 %broadcast_multiply_fusion = f32[2,384,128]{2,1,0:T(8,128)} fusion(f32[2,384,128]{2,1,0:T(8,128)} %shard_map.46, f32[384]{0:T(512)S(1)} %fusion.3), kind=kLoop, calls=%fused_computation | loop fusion | flops 98304 | bytes 787968 | tf_op jit(solution)/shard_map/mul | solution.py:470
  (1 shorter events, 0.0 us)

commit v4 on v3

--- a/solution.py
+++ b/solution.py
@@ -423,7 +423,7 @@
     pairs = lax.axis_size("slab") // 2
     result = pl.pallas_call(
         functools.partial(kernel, lax.axis_size("slab")),
-        out_shape=jax.ShapeDtypeStruct((2, rows, cols), F32),
+        out_shape=pltpu.VMEM((2, rows, cols), F32),
         in_specs=[pl.BlockSpec(memory_space=pltpu.HBM)] * 3 + [pl.BlockSpec(memory_space=pltpu.SMEM)],
         out_specs=pl.BlockSpec(memory_space=pltpu.VMEM),
         scratch_shapes=[

time: 31.9 us -> 30.2 us (0.947)
  other arithmetic: 1.87 us -> 0.87 us
  Pallas kernels: 29.2 us -> 28.5 us
    mul x1, other arithmetic: 1.86 us -> 0.87 us  [body(): return result * live[None, :, None]]
    pallas_call x1, Pallas kernels: 29.2 us -> 28.5 us  [body(): pl.pallas_call(functools.partial(kernel, lax.axis_size('slab')), out_shap...]
where the time goes in v4:
time: 30.2 us; the launch traced here: 30 us
  Pallas kernels  28.5 us (94%)
  other arithmetic  0.87 us (3%)
  between operations  0.67 us (2%)
    pallas_call x1, Pallas kernels, body(): pl.pallas_call(functools.partial(kernel, lax.axis_size('slab')), out_shap...  28.5 us
    mul x1, other arithmetic, body(): return result * live[None, :, None]  0.87 us

profile of v4, /device:TPU:5, one launch (start us, length us, event | category | flops | bytes accessed | tf_op | source)
XLA Modules:
  0.0 30.0 jit_solution(8987445524355221373)
XLA Ops:
  0.7 28.5 %shard_map.46 = f32[2,384,128]{2,1,0:T(8,128)S(1)} custom-call(bf16[2,384,768]{2,1,0:T(8,128)(2,1)} %green_hbm.1, bf16[2,128,128]{2,1,0:T(8,128)(2,1)} %couple_hbm.1, bf16[2,384,128]{2,1,0:T(8,128)(2,1)} %source_hbm.1, s32[1]{0:T(128)S(6)} %copy.5.interior_ref), custom_call_target="tpu_custom_call" | custom-call | tf_op jit(solution)/shard_map/pallas_call | solution.py:424
  29.1 0.9 %broadcast_multiply_fusion = f32[2,384,128]{2,1,0:T(8,128)} fusion(f32[2,384,128]{2,1,0:T(8,128)S(1)} %shard_map.46, f32[384]{0:T(512)S(1)} %fusion.3), kind=kLoop, calls=%fused_computation | loop fusion | flops 98304 | bytes 787968 | tf_op jit(solution)/shard_map/mul | solution.py:470
  (1 shorter events, 0.0 us)

commit v5 on v4

--- a/solution.py
+++ b/solution.py
@@ -266,32 +266,32 @@
         couple_now = next_coupling()
         back = dot(block(0, tail), couple_now)
         if not even:
-            out_1[...] = back
+            out_1[...] = back.astype(BF16)
             push(out_1, BACK_B, S_1, s - 1, 0)
         previous_coupling()
         adj_real, adj_imag = previous_adjoint()
         adjoint = embed(adj_real, adj_imag)
         cross = dot(block(0, head), jnp.concatenate([adj_real, adj_imag], axis=0))
         if not even:
-            out_2[...] = cross
+            out_2[...] = cross.astype(BF16)
             push(out_2, CROSS_B, S_2, s - 1, 0)
             couple_map = embed(couple_now[:w], couple_now[w:])
         else:
             couple_map = embed(couple_now[:w], couple_now[w:])
             arrived(BACK_B)
             back_own = wide_map(back)
-            ship_map[...] = apply_wide(back_own, back_b[...]).astype(BF16)
+            ship_map[...] = apply_rounded(back_own, back_b[...]).astype(BF16)
             far_push(ship_map, back_maps, 3, earlier_map)
-            back_far = wide_map(back_b[...])
+            back_far = embed(back_b[:w], back_b[w:])
             arrived(CROSS_B)
             arrived(MAP_A)
-            cross_far = wide_map(cross_b[...])
-            cross_two_f = apply_wide(cross_far, map_a[...])
+            cross_far = embed(cross_b[:w], cross_b[w:])
+            cross_two_f = apply_exact(cross_far, map_a[...])
             cross_two = wide_map(cross_two_f)
             cross_all = wide_map(cross + apply_wide(back_own, cross_two_f))
             arrived(FIRST_B)
             arrived(TERM_A)
-            term_b = first_b[...] + apply_rounded(cross_far, term_a[...])
+            term_b = first_b[...] + dot(cross_far, term_a[...])
             term = first + apply_wide(back_own, term_b)
             run(totals, total_maps, 0, 0, pair, 1)
             before = running[...]
@@ -315,7 +315,7 @@
                 after[...] = follow.astype(BF16)
                 push(after, AFTER, S_0, s + 1, 0)
 
-            up_out[...] = apply_exact(couple_map, after_own + apply_wide(back_far, follow)).astype(BF16)
+            up_out[...] = apply_exact(couple_map, after_own + apply_exact(back_far, follow)).astype(BF16)
             push(up_out, UPPER, S_UPPER, s, 1)
             add_product(pairwise(up_out), tail, False)
             sent(low_out, S_LOWER)
@@ -355,8 +355,8 @@
         forward = dot(block(rows - w, head), jnp.concatenate([adj_real, adj_imag], axis=0))
         if even:
             out_0[...] = forward
+            push(out_0, MAP_A, S_1, s + 1, 1)
             push(out_0, MAP_A, S_0, s, 0)
-            push(out_0, MAP_A, S_1, s + 1, 1)
         else:
             own = wide_map(forward)
         turned = wide_map(dot(block(rows - w, tail), next_coupling()))
@@ -435,8 +435,8 @@
             small,
             square,
             small,
-            square,
-            square,
+            pltpu.VMEM((2 * w, w), BF16),
+            pltpu.VMEM((2 * w, w), BF16),
             block,
             small,
             small,
@@ -444,8 +444,8 @@
             small,
             small,
             block,
-            block,
-            square,
+            pltpu.VMEM((2 * w, w), BF16),
+            pltpu.VMEM((2 * w, w), BF16),
             small,
             small,
             small,

time: 30.2 us -> 30.2 us (level)
  no operation moved by 1% of the time
where the time goes in v5:
time: 30.2 us; the launch traced here: 30 us
  Pallas kernels  28.5 us (94%)
  other arithmetic  0.87 us (3%)
  between operations  0.67 us (2%)
    pallas_call x1, Pallas kernels, body(): pl.pallas_call(functools.partial(kernel, lax.axis_size('slab')), out_shap...  28.5 us
    mul x1, other arithmetic, body(): return result * live[None, :, None]  0.87 us

profile of v5, /device:TPU:5, one launch (start us, length us, event | category | flops | bytes accessed | tf_op | source)
XLA Modules:
  0.0 30.0 jit_solution(12056624287868759430)
XLA Ops:
  0.7 28.5 %shard_map.46 = f32[2,384,128]{2,1,0:T(8,128)S(1)} custom-call(bf16[2,384,768]{2,1,0:T(8,128)(2,1)} %green_hbm.1, bf16[2,128,128]{2,1,0:T(8,128)(2,1)} %couple_hbm.1, bf16[2,384,128]{2,1,0:T(8,128)(2,1)} %source_hbm.1, s32[1]{0:T(128)S(6)} %copy.5.interior_ref), custom_call_target="tpu_custom_call" | custom-call | tf_op jit(solution)/shard_map/pallas_call | solution.py:424
  29.1 0.9 %broadcast_multiply_fusion = f32[2,384,128]{2,1,0:T(8,128)} fusion(f32[2,384,128]{2,1,0:T(8,128)S(1)} %shard_map.46, f32[384]{0:T(512)S(1)} %fusion.3), kind=kLoop, calls=%fused_computation | loop fusion | flops 98304 | bytes 787968 | tf_op jit(solution)/shard_map/mul | solution.py:470
  (1 shorter events, 0.0 us)

commit v6 on v4

--- a/solution.py
+++ b/solution.py
@@ -191,22 +191,21 @@
             [(ref[0].astype(F32) * live).astype(BF16), (ref[1].astype(F32) * live).astype(BF16)], axis=1
         )
 
-    def add_product(x, columns, first):
-        by_real = dot(green[0, :, columns], x)
-        by_imag = dot(green[1, :, columns], x)
+    def add_product(x, columns, first, span=slice(None)):
+        by_real = dot(green[0, span, columns], x)
+        by_imag = dot(green[1, span, columns], x)
         real = by_real[:, :cols] - by_imag[:, cols:]
         imag = by_real[:, cols:] + by_imag[:, :cols]
         if first:
             out_ref[0], out_ref[1] = real, imag
         else:
-            out_ref[0] += real
-            out_ref[1] += imag
+            out_ref[0, span, :] += real
+            out_ref[1, span, :] += imag
 
     loads[0].wait()
     loads[1].wait()
     add_product(injected(source, r), pl.ds(pl.multiple_of(r * rows, w), rows), True)
     arrived(SOURCE)
-    add_product(injected(source_in, 1 - r), pl.ds(pl.multiple_of((1 - r) * rows, w), rows), False)
 
     loads[2].wait()
     head, tail = slice(0, w), slice(width - w, width)
@@ -253,6 +252,9 @@
             ref[...] = jnp.zeros_like(ref)
 
     def row_zero(even):
+        there = slice(rows, 2 * rows)
+        injection = injected(source_in, 1)
+        add_product(injection, there, False, slice(0, w))
         first = surface(0)
         edge_out[...] = first.astype(BF16)
 
@@ -263,6 +265,7 @@
         if not even:
             out_0[...] = first
             push(out_0, FIRST_B, S_0, s - 1, 0)
+        add_product(injection, there, False, slice(w, rows))
         couple_now = next_coupling()
         back = dot(block(0, tail), couple_now)
         if not even:
@@ -349,6 +352,7 @@
             sent(out_2, S_2)
 
     def row_one(even):
+        add_product(injected(source_in, 0), slice(0, rows), False)
         last = surface(rows - w)
         previous_coupling()
         adj_real, adj_imag = previous_adjoint()

time: 30.2 us -> 30.2 us (level)
  no operation moved by 1% of the time
where the time goes in v6:
time: 30.2 us; the launch traced here: 30 us
  Pallas kernels  28.5 us (94%)
  other arithmetic  0.87 us (3%)
  between operations  0.67 us (2%)
    pallas_call x1, Pallas kernels, body(): pl.pallas_call(functools.partial(kernel, lax.axis_size('slab')), out_shap...  28.5 us
    mul x1, other arithmetic, body(): return result * live[None, :, None]  0.87 us

profile of v6, /device:TPU:5, one launch (start us, length us, event | category | flops | bytes accessed | tf_op | source)
XLA Modules:
  0.0 30.0 jit_solution(7278975612778734128)
XLA Ops:
  0.7 28.5 %shard_map.46 = f32[2,384,128]{2,1,0:T(8,128)S(1)} custom-call(bf16[2,384,768]{2,1,0:T(8,128)(2,1)} %green_hbm.1, bf16[2,128,128]{2,1,0:T(8,128)(2,1)} %couple_hbm.1, bf16[2,384,128]{2,1,0:T(8,128)(2,1)} %source_hbm.1, s32[1]{0:T(128)S(6)} %copy.5.interior_ref), custom_call_target="tpu_custom_call" | custom-call | tf_op jit(solution)/shard_map/pallas_call | solution.py:428
  29.1 0.9 %broadcast_multiply_fusion = f32[2,384,128]{2,1,0:T(8,128)} fusion(f32[2,384,128]{2,1,0:T(8,128)S(1)} %shard_map.46, f32[384]{0:T(512)S(1)} %fusion.3), kind=kLoop, calls=%fused_computation | loop fusion | flops 98304 | bytes 787968 | tf_op jit(solution)/shard_map/mul | solution.py:474
  (1 shorter events, 0.0 us)

commit v7 on v6

--- a/solution.py
+++ b/solution.py
@@ -378,11 +378,11 @@
         else:
             arrived(MAP_A)
             ship_map[...] = apply_wide(own, map_a[...]).astype(BF16)
-            far_push(ship_map, total_maps, 1, later_map)
             near = wide_map(map_a[...])
             arrived(TERM_A)
             ship[...] = (term + apply_rounded(own, term_a[...])).astype(BF16)
             far_push(ship, totals, 0, later_term)
+            far_push(ship_map, total_maps, 1, later_map)
             no_state(state, pair > 0, STATE)
             before = state[...]
             inner = term_a[...].astype(F32) + apply_rounded(near, before)

time: 30.2 us -> 30.9 us (1.023)
  Pallas kernels: 28.5 us -> 29.2 us
    pallas_call x1, Pallas kernels: 28.5 us -> 29.2 us  [body(): pl.pallas_call(functools.partial(kernel, lax.axis_size('slab')), out_shap...]
where the time goes in v7:
time: 30.9 us; the launch traced here: 30.7 us
  Pallas kernels  29.2 us (94%)
  other arithmetic  0.87 us (3%)
  between operations  0.67 us (2%)
    pallas_call x1, Pallas kernels, body(): pl.pallas_call(functools.partial(kernel, lax.axis_size('slab')), out_shap...  29.2 us
    mul x1, other arithmetic, body(): return result * live[None, :, None]  0.87 us

profile of v7, /device:TPU:5, one launch (start us, length us, event | category | flops | bytes accessed | tf_op | source)
XLA Modules:
  0.0 30.7 jit_solution(14720637824029207354)
XLA Ops:
  0.7 29.2 %shard_map.46 = f32[2,384,128]{2,1,0:T(8,128)S(1)} custom-call(bf16[2,384,768]{2,1,0:T(8,128)(2,1)} %green_hbm.1, bf16[2,128,128]{2,1,0:T(8,128)(2,1)} %couple_hbm.1, bf16[2,384,128]{2,1,0:T(8,128)(2,1)} %source_hbm.1, s32[1]{0:T(128)S(6)} %copy.5.interior_ref), custom_call_target="tpu_custom_call" | custom-call | tf_op jit(solution)/shard_map/pallas_call | solution.py:428
  29.9 0.9 %broadcast_multiply_fusion = f32[2,384,128]{2,1,0:T(8,128)} fusion(f32[2,384,128]{2,1,0:T(8,128)S(1)} %shard_map.46, f32[384]{0:T(512)S(1)} %fusion.3), kind=kLoop, calls=%fused_computation | loop fusion | flops 98304 | bytes 787968 | tf_op jit(solution)/shard_map/mul | solution.py:474
  (1 shorter events, 0.0 us)
